TPU v7x, 128 devices: a whole 4x4x4 slice. The times are simulated.
128 devices in a mesh: pix: 16 (over x, y_hi, core), tm: 8 (over y_lo, z).
Axes of the slice: x: 4, y: 4 (y_hi: 2, y_lo: 2; y = y_hi * 2 + y_lo), z: 4, core: 2. Of those that a mesh axis runs over, the one named last changes fastest.
Arguments:
- movie: bfloat16 [32768, 8192], P('pix', 'tm'), may hold values from -6 to 6
- offsets: int32 [8], replicated, may hold values from -129 to 129, as said below
- spatial: bfloat16 [512, 32768], P('tm', 'pix'), may hold values from -6 to 6
- temporal: bfloat16 [512, 8192], P('pix', 'tm'), may hold values from -6 to 6
- step_spatial: float32 [512], replicated, may hold values from 0.3 to 1
- step_temporal: float32 [512], replicated, may hold values from 0.3 to 1
- thresh_spatial: float32 [512], replicated, may hold values from 0.01 to 0.2
- thresh_temporal: float32 [512], replicated, may hold values from 0.01 to 0.2
Outputs:
- spatial_out: bfloat16 [512, 32768], P('tm', 'pix')
- temporal_out: bfloat16 [512, 8192], P('pix', 'tm')
Inputs may be any that keep to these rules, and one draw needn't show every extreme that they name: `offsets`: every offset is a nonzero pixel step of magnitude at most 129; both 129 and -129 occur among them.
All inputs are finite; a program needn't handle non-finite values.
Results may differ from a plain program's by a relative error of at most 0.0052.
Values may be sent and summed in bfloat16 or wider, within the bound.
No kernel may reach another device: no remote copies, remote signals or barrier semaphores. Data moves between devices by JAX's collectives and lax.ppermute only.
A program may use at most 64 MiB of HBM per device.

v0:
```python
import math
import jax
import jax.numpy as jnp
from jax import lax
from jax.sharding import PartitionSpec as P

HALO = 129
NBR = 8
ROUNDS = 2


def padded_2(array, sides, width):
    for axis, dim in sides:
        size, length = (lax.axis_size(axis), array.shape[dim])
        up = [(i, (i + 1) % size) for i in range(size - 1)]
        down = [(j, i) for i, j in up]
        last = lax.slice_in_dim(array, length - width, length, axis=dim)
        initial = lax.slice_in_dim(array, 0, width, axis=dim)
        before = lax.ppermute(last, axis, up)
        after = lax.ppermute(initial, axis, down)
        array = jnp.concatenate([before, array, after], axis=dim)
    return array


def soften(values, limit):
    return values - jnp.clip(values, -limit, limit)


def contrast(movie, offsets):
    count = movie.shape[0]
    padded = padded_2(movie, (("pix", 0),), HALO)
    total = jnp.zeros(movie.shape, jnp.float32)
    for neighbour in range(NBR):
        begin = HALO + offsets[neighbour]
        shifted = lax.dynamic_slice_in_dim(padded, begin, count, 0)
        total = total + shifted.astype(jnp.float32)
    return (movie.astype(jnp.float32) - total / NBR).astype(jnp.bfloat16)


def residual(contrasted, spatial_full, temporal_full, rank):
    model = lax.dot_general(
        spatial_full, temporal_full, (((0,), (0,)), ((), ())), preferred_element_type=jnp.float32
    )
    return (contrasted.astype(jnp.float32) - model * (1.0 / math.sqrt(rank))).astype(jnp.bfloat16)


def per_device(
    movie, offsets, spatial, temporal, step_spatial, step_temporal, thresh_spatial, thresh_temporal
):
    spatial_rows = spatial.shape[0]
    temporal_rows = temporal.shape[0]
    rank = spatial_rows * lax.axis_size("tm")
    pixels = movie.shape[0] * lax.axis_size("pix")
    frames = movie.shape[1] * lax.axis_size("tm")
    contrasted = contrast(movie, offsets)
    spatial_full = lax.all_gather(spatial, "tm", axis=0, tiled=True)
    temporal_full = lax.all_gather(temporal, "pix", axis=0, tiled=True)
    coef_temporal = step_temporal * (math.sqrt(rank) / pixels)
    coef_spatial = step_spatial * (math.sqrt(rank) / frames)
    temporal_first = lax.axis_index("pix") * temporal_rows
    spatial_first = lax.axis_index("tm") * spatial_rows
    for turn in range(ROUNDS):
        errors = residual(contrasted, spatial_full, temporal_full, rank)
        grad_temporal = lax.psum(
            jnp.dot(spatial_full, errors, preferred_element_type=jnp.float32), "pix"
        )
        temporal_full = soften(
            temporal_full.astype(jnp.float32) + coef_temporal[:, None] * grad_temporal,
            thresh_temporal[:, None],
        ).astype(jnp.bfloat16)
        errors = residual(contrasted, spatial_full, temporal_full, rank)
        partial_spatial = lax.dot_general(
            temporal_full, errors, (((1,), (1,)), ((), ())), preferred_element_type=jnp.float32
        )
        grad_spatial = lax.psum(partial_spatial, "tm")
        spatial_full = soften(
            spatial_full.astype(jnp.float32) + coef_spatial[:, None] * grad_spatial,
            thresh_spatial[:, None],
        ).astype(jnp.bfloat16)
    spatial_out = lax.dynamic_slice_in_dim(spatial_full, spatial_first, spatial_rows, 0)
    temporal_out = lax.dynamic_slice_in_dim(temporal_full, temporal_first, temporal_rows, 0)
    return (spatial_out, temporal_out)


def solution(mesh):
    placed = (P("pix", "tm"), P(), P("tm", "pix"), P("pix", "tm"), P(), P(), P(), P())
    return jax.shard_map(
        per_device,
        mesh=mesh,
        in_specs=placed,
        out_specs=(P("tm", "pix"), P("pix", "tm")),
        check_vma=False,
    )
```

profile of v0, /device:TPU:1, one launch (start us, length us, event | category | flops | bytes accessed | tf_op | source)
XLA Modules:
  0.0 656.8 jit_solution(3651057395726386924)
XLA Ops:
  7.2 0.7 all-gather.5.cloned.1.call-update
  7.9 0.7 all-gather.3.cloned.1.call-update
  8.7 1.1 fusion.12
  9.8 6.2 collective-permute-start
  16.0 1.9 collective-permute-start.1
  18.0 1.6 fusion.13
  29.6 24.4 %concatenate.3 = bf16[2306,1024]{1,0:T(8,128)(2,1)} concatenate(bf16[129,1024]{1,0:T(8,128)(2,1)S(1)} %collective-permute-done, bf16[2048,1024]{1,0:T(8,128)(2,1)} %param.8, bf16[129,1024]{1,0:T(8,128)(2,1)S(1)} %collective-permute-done.1), dimensions={0} | concatenate | bytes 9445376 | tf_op jit(solution)/shard_map/concatenate | solution.py:21
  54.0 19.6 %subtract_convert_fusion = bf16[2048,1024]{1,0:T(8,128)(2,1)} fusion(bf16[2048,1024]{1,0:T(8,128)(2,1)} %param.8, bf16[2306,1024]{1,0:T(8,128)(2,1)} %concatenate.3, s32[]{:T(128)S(6)} %select_n.37, s32[]{:T(128)S(6)} %select_n.36, s32[]{:T(128)S(6)} %select_n.35, s32[]{:T(128)S(6)} %select_n.34, s32[]{:T(128)S(6)} %select_n.33, s32[]{:T(128)S(6)} %select_n.32, ...), kind=kLoop, calls=%fused_computation.8 | loop fusion | flops 39845888 | bytes 41943072 | tf_op jit(solution)/shard_map/convert_element_type | solution.py:37
  73.6 21.8 %all-gather.3.cloned.1.call-done = bf16[512,2048]{1,0:T(8,128)(2,1)} async-done(((bf16[64,2048]{1,0:T(8,128)(2,1)}), bf16[512,2048]{1,0:T(8,128)(2,1)}) %all-gather.3.cloned.1.call-update) | async-done | bytes 2097168 | tf_op jit(solution)/shard_map/all_gather | solution.py:56
  95.5 9.9 %convolution_bitcast_fusion = f32[512,1024]{0,1:T(8,128)} fusion(bf16[512,2048]{1,0:T(8,128)(2,1)} %all-gather.3.cloned.1.call-done, bf16[2048,1024]{1,0:T(8,128)(2,1)} %subtract_convert_fusion, bf16[512,1024]{1,0:T(8,128)(2,1)} %all-gather.5.cloned.1.call-done), kind=kOutput, calls=%fused_computation.12 | convolution fusion | flops 4303355904 | bytes 9437184 | tf_op jit(solution)/shard_map/dot_general | solution.py:65
  106.2 147.7 %all-reduce.5.cloned.1.call-done = f32[512,1024]{0,1:T(8,128)} async-done(((f32[512,1024]{0,1:T(8,128)}), f32[512,1024]{0,1:T(8,128)}) %all-reduce.5.cloned.1.call-update) | async-done | bytes 2097168 | tf_op jit(solution)/shard_map/psum | solution.py:64
  254.0 2.1 subtract_convert_fusion.3
  256.0 9.8 %fusion.6 = f32[512,2048]{1,0:T(8,128)} fusion(bf16[512,1024]{0,1:T(8,128)(2,1)S(1)} %subtract_convert_fusion.3, bf16[2048,1024]{1,0:T(8,128)(2,1)} %subtract_convert_fusion, bf16[512,2048]{1,0:T(8,128)(2,1)} %all-gather.3.cloned.1.call-done), kind=kOutput, calls=%fused_computation.15 | convolution fusion | flops 4303355904 | bytes 11534336 | tf_op jit(solution)/shard_map/dot_general | solution.py:72
  265.9 0.6 copy-done.2
  266.5 106.3 %all-reduce.7.cloned.1.call-done = f32[512,2048]{1,0:T(8,128)} async-done(((f32[512,2048]{1,0:T(8,128)}), f32[512,2048]{1,0:T(8,128)}) %all-reduce.7.cloned.1.call-update) | async-done | bytes 4194320 | tf_op jit(solution)/shard_map/psum | solution.py:75
  372.9 3.9 subtract_convert_fusion.1
  376.7 8.5 %fusion.5 = f32[512,1024]{0,1:T(8,128)} fusion(bf16[512,2048]{1,0:T(8,128)(2,1)S(1)} %subtract_convert_fusion.1, bf16[2048,1024]{1,0:T(8,128)(2,1)} %subtract_convert_fusion, bf16[512,1024]{0,1:T(8,128)(2,1)S(1)} %subtract_convert_fusion.3), kind=kOutput, calls=%fused_computation.14 | convolution fusion | flops 4303355904 | bytes 9437184 | tf_op jit(solution)/shard_map/dot_general | solution.py:65
  385.5 142.7 %all-reduce.9.cloned.1.call-done = f32[512,1024]{0,1:T(8,128)} async-done(((f32[512,1024]{0,1:T(8,128)}), f32[512,1024]{0,1:T(8,128)}) %all-reduce.9.cloned.1.call-update) | async-done | bytes 2097168 | tf_op jit(solution)/shard_map/psum | solution.py:64
  528.2 3.0 subtract_convert_fusion.2
  531.3 9.7 %fusion.4 = f32[512,2048]{1,0:T(8,128)} fusion(bf16[512,1024]{0,1:T(8,128)(2,1)} %subtract_convert_fusion.2, bf16[2048,1024]{1,0:T(8,128)(2,1)} %subtract_convert_fusion, bf16[512,2048]{1,0:T(8,128)(2,1)S(1)} %subtract_convert_fusion.1), kind=kOutput, calls=%fused_computation.13 | convolution fusion | flops 4303355904 | bytes 11534336 | tf_op jit(solution)/shard_map/dot_general | solution.py:72
  541.3 1.1 constant_dynamic-slice_fusion
  542.3 0.8 copy.15
  543.1 105.0 %all-reduce.11.cloned.1.call-done = f32[512,2048]{1,0:T(8,128)} async-done(((f32[512,2048]{1,0:T(8,128)}), f32[512,2048]{1,0:T(8,128)}) %all-reduce.11.cloned.1.call-update) | async-done | bytes 4194320 | tf_op jit(solution)/shard_map/psum | solution.py:75
  648.1 1.9 subtract_convert_fusion.4
  (30 shorter events, 1.5 us)
Async XLA Ops:
  7.2 66.4 %all-gather.5.cloned.1.call-start = ((), (), s32[]{:S(2)}) async-start(), calls=%async_computation.1 | async-start | bytes 1114112 | tf_op jit(solution)/shard_map/all_gather | solution.py:57
  7.9 87.6 %all-gather.3.cloned.1.call-start = ((), (), s32[]{:S(2)}) async-start(), calls=%async_computation | async-start | bytes 2359296 | tf_op jit(solution)/shard_map/all_gather | solution.py:56
  8.6 245.3 %all-reduce.5.cloned.1.call-start = ((), (), s32[]{:S(2)}) async-start(), calls=%async_computation.2 | async-start | bytes 4194304 | tf_op jit(solution)/shard_map/psum | solution.py:64
  9.8 19.8 %collective-permute-start = (bf16[129,1024]{1,0:T(8,128)(2,1)S(1)}, bf16[129,1024]{1,0:T(8,128)(2,1)S(1)}, u32[]{:S(2)}, u32[]{:S(2)}) collective-permute-start(bf16[129,1024]{1,0:T(8,128)(2,1)S(1)} %get-tuple-element.7), channel_id=1, source_target_pairs={{0,8},{8,16},{16,24},{24,32},{32,40},{40,48},{48,56},{56,64},{64,7... | collective-permute-start | bytes 792584 | tf_op jit(solution)/shard_map/ppermute | solution.py:19
  16.0 13.5 %collective-permute-start.1 = (bf16[129,1024]{1,0:T(8,128)(2,1)S(1)}, bf16[129,1024]{1,0:T(8,128)(2,1)S(1)}, u32[]{:S(2)}, u32[]{:S(2)}) collective-permute-start(bf16[129,1024]{1,0:T(8,128)(2,1)S(1)} %get-tuple-element.6), channel_id=1, source_target_pairs={{8,0},{16,8},{24,16},{32,24},{40,32},{48,40},{56,48},{64,56},{72,6... | collective-permute-start | bytes 792584 | tf_op jit(solution)/shard_map/ppermute | solution.py:20
  73.6 32.1 %copy-start.1 = (f32[512]{0:T(512)S(1)}, f32[512]{0:T(512)}, u32[]{:S(2)}) copy-start(f32[512]{0:T(512)} %param.15) | copy-start | bytes 6148
  73.6 32.1 %copy-start.3 = (f32[512]{0:T(512)S(1)}, f32[512]{0:T(512)}, u32[]{:S(2)}) copy-start(f32[512]{0:T(512)} %param.13) | copy-start | bytes 6148
  73.6 32.1 %copy-start = (bf16[512,1024]{1,0:T(8,128)(2,1)S(1)}, bf16[512,1024]{1,0:T(8,128)(2,1)}, u32[]{:S(2)}) copy-start(bf16[512,1024]{1,0:T(8,128)(2,1)} %all-gather.5.cloned.1.call-done) | copy-start | bytes 3145732
  105.4 267.5 %all-reduce.7.cloned.1.call-start = ((), (), s32[]{:S(2)}) async-start(), calls=%async_computation.3 | async-start | bytes 8388608 | tf_op jit(solution)/shard_map/psum | solution.py:75
  265.8 0.7 copy-start.2
  265.8 0.7 copy-start.4
  265.9 262.4 %all-reduce.9.cloned.1.call-start = ((), (), s32[]{:S(2)}) async-start(), calls=%async_computation.4 | async-start | bytes 4194304 | tf_op jit(solution)/shard_map/psum | solution.py:64
  385.3 262.8 %all-reduce.11.cloned.1.call-start = ((), (), s32[]{:S(2)}) async-start(), calls=%async_computation.5 | async-start | bytes 8388608 | tf_op jit(solution)/shard_map/psum | solution.py:75
Sparse Core Ops, SparseCore 0:
  10.4 48.5 all-gather.4
  60.6 34.7 all-gather.2
  105.5 148.3 all-reduce.4
  266.0 106.8 all-reduce.6
  385.4 142.8 all-reduce.8
  541.1 106.8 all-reduce.10
where the time goes:
time: 658 us; the launch traced here: 657 us
  waiting for transfers between devices  525 us (80%)
  matrix products  37.9 us (6%)
  local copies, waits for them, and re-layouts  30.4 us (5%)
  other arithmetic  30.4 us (5%)
  between operations  24.2 us (4%)
  starting transfers between devices  8.77 us (1%)
    psum x2, waiting for transfers between devices, per_device(): lax.psum(jnp.dot(spatial_full, errors, preferred_element_type=jnp.float32...  290 us
    psum x2, waiting for transfers between devices, per_device(): grad_spatial = lax.psum(partial_spatial, 'tm')  211 us
    concatenate x1, local copies, waits for them, and re-layouts, padded_2(): array = jnp.concatenate([before, array, after], axis=dim)  24.4 us
    all_gather x1, waiting for transfers between devices, per_device(): spatial_full = lax.all_gather(spatial, 'tm', axis=0, tiled=True)  21.8 us
    convert_element_type x1, other arithmetic, contrast(): return (movie.astype(jnp.float32) - total / NBR).astype(jnp.bfloat16)  19.6 us
    dot_general x2, matrix products, per_device(): lax.dot_general(temporal_full, errors, (((1,), (1,)), ((), ())), preferre...  19.5 us
    dot_general x2, matrix products, per_device(): jnp.dot(spatial_full, errors, preferred_element_type=jnp.float32)  18.4 us
  transfers between devices with their start and end apart: 8, of which 5 were waited for; matrix products, arithmetic and copies ran while one was open for 8% of the time, Pallas kernels for 0%

commit v1 on v0

--- a/solution.py
+++ b/solution.py
@@ -53,7 +53,9 @@
     pixels = movie.shape[0] * lax.axis_size("pix")
     frames = movie.shape[1] * lax.axis_size("tm")
     contrasted = contrast(movie, offsets)
-    spatial_full = lax.all_gather(spatial, "tm", axis=0, tiled=True)
+    spatial_full = jnp.concatenate(
+        lax.all_to_all(jnp.stack([spatial] * lax.axis_size("tm")), "tm", 0, 0), axis=0
+    )
     temporal_full = lax.all_gather(temporal, "pix", axis=0, tiled=True)
     coef_temporal = step_temporal * (math.sqrt(rank) / pixels)
     coef_spatial = step_spatial * (math.sqrt(rank) / frames)

time: 658 us -> 655 us (level)
  waiting for transfers between devices: 525 us -> 514 us
    all_gather x1 -> x0, waiting for transfers between devices: 21.8 us -> none  [per_device(): spatial_full = lax.all_gather(spatial, 'tm', axis=0, tiled=True)]
    ppermute x1, waiting for transfers between devices: 0.01 us -> 13.6 us  [padded_2(): before = lax.ppermute(last, axis, up)]
    all_to_all x0 -> x1, starting transfers between devices: none -> 6.88 us  [per_device(): lax.all_to_all(jnp.stack([spatial] * lax.axis_size('tm')), 'tm', 0, 0)]
where the time goes in v1:
time: 655 us; the launch traced here: 654 us
  waiting for transfers between devices  514 us (78%)
  matrix products  37.3 us (6%)
  local copies, waits for them, and re-layouts  32.8 us (5%)
  other arithmetic  31.2 us (5%)
  between operations  24 us (4%)
  starting transfers between devices  14.8 us (2%)
    psum x2, waiting for transfers between devices, per_device(): lax.psum(jnp.dot(spatial_full, errors, preferred_element_type=jnp.float32...  288 us
    psum x2, waiting for transfers between devices, per_device(): grad_spatial = lax.psum(partial_spatial, 'tm')  211 us
    concatenate x1, local copies, waits for them, and re-layouts, padded_2(): array = jnp.concatenate([before, array, after], axis=dim)  24.5 us
    convert_element_type x1, other arithmetic, contrast(): return (movie.astype(jnp.float32) - total / NBR).astype(jnp.bfloat16)  19.4 us
    dot_general x2, matrix products, per_device(): lax.dot_general(temporal_full, errors, (((1,), (1,)), ((), ())), preferre...  18.8 us
    dot_general x2, matrix products, per_device(): jnp.dot(spatial_full, errors, preferred_element_type=jnp.float32)  18.4 us
    ppermute x1, waiting for transfers between devices, padded_2(): before = lax.ppermute(last, axis, up)  13.6 us
  transfers between devices with their start and end apart: 8, of which 5 were waited for; matrix products, arithmetic and copies ran while one was open for 8% of the time, Pallas kernels for 0%

profile of v1, /device:TPU:1, one launch (start us, length us, event | category | flops | bytes accessed | tf_op | source)
XLA Modules:
  0.0 653.6 jit_solution(2984493237017938894)
XLA Ops:
  7.2 0.7 all-gather.2.cloned.1.call-update
  7.9 2.5 stack.2
  10.4 6.9 %all-to-all-start = ((bf16[8,64,2048]{2,1,0:T(8,128)(2,1)}), bf16[8,64,2048]{2,1,0:T(8,128)(2,1)S(1)}, u32[]{:S(2)}, u32[]{:S(2)}) async-start(bf16[8,64,2048]{2,1,0:T(8,128)(2,1)} %stack.2), calls=%async_computation | async-start | bytes 4194304 | tf_op jit(solution)/shard_map/all_to_all | solution.py:57
  17.4 1.1 fusion.12
  18.5 5.4 collective-permute-start
  23.9 1.9 collective-permute-start.1
  36.6 13.6 %collective-permute-done = bf16[129,1024]{1,0:T(8,128)(2,1)S(1)} collective-permute-done((bf16[129,1024]{1,0:T(8,128)(2,1)S(1)}, bf16[129,1024]{1,0:T(8,128)(2,1)S(1)}, u32[]{:S(2)}, u32[]{:S(2)}) %collective-permute-start) | collective-permute-done | bytes 264224 | tf_op jit(solution)/shard_map/ppermute | solution.py:19
  50.1 24.5 %concatenate.3 = bf16[2306,1024]{1,0:T(8,128)(2,1)} concatenate(bf16[129,1024]{1,0:T(8,128)(2,1)S(1)} %collective-permute-done, bf16[2048,1024]{1,0:T(8,128)(2,1)} %param.8, bf16[129,1024]{1,0:T(8,128)(2,1)S(1)} %collective-permute-done.1), dimensions={0} | concatenate | bytes 9445376 | tf_op jit(solution)/shard_map/concatenate | solution.py:21
  74.6 19.4 %subtract_convert_fusion = bf16[2048,1024]{1,0:T(8,128)(2,1)} fusion(bf16[2048,1024]{1,0:T(8,128)(2,1)} %param.8, bf16[2306,1024]{1,0:T(8,128)(2,1)} %concatenate.3, s32[]{:T(128)S(6)} %select_n.37, s32[]{:T(128)S(6)} %select_n.36, s32[]{:T(128)S(6)} %select_n.35, s32[]{:T(128)S(6)} %select_n.34, s32[]{:T(128)S(6)} %select_n.33, s32[]{:T(128)S(6)} %select_n.32, ...), kind=kLoop, calls=%fused_computation.8 | loop fusion | flops 39845888 | bytes 41943072 | tf_op jit(solution)/shard_map/convert_element_type | solution.py:37
  94.1 8.8 %convolution_bitcast_fusion = f32[512,1024]{0,1:T(8,128)} fusion(bf16[512,2048]{1,0:T(8,128)(2,1)S(1)} %bitcast.36, bf16[2048,1024]{1,0:T(8,128)(2,1)} %subtract_convert_fusion, bf16[512,1024]{1,0:T(8,128)(2,1)} %all-gather.2.cloned.1.call-done), kind=kOutput, calls=%fused_computation.12 | convolution fusion | flops 4303355904 | bytes 9437184 | tf_op jit(solution)/shard_map/dot_general | solution.py:67
  103.1 1.3 copy.13
  104.5 145.3 %all-reduce.5.cloned.1.call-done = f32[512,1024]{0,1:T(8,128)} async-done(((f32[512,1024]{0,1:T(8,128)}), f32[512,1024]{0,1:T(8,128)}) %all-reduce.5.cloned.1.call-update) | async-done | bytes 2097168 | tf_op jit(solution)/shard_map/psum | solution.py:66
  249.8 2.3 subtract_convert_fusion.3
  252.1 9.2 %fusion.6 = f32[512,2048]{1,0:T(8,128)} fusion(bf16[512,1024]{0,1:T(8,128)(2,1)S(1)} %subtract_convert_fusion.3, bf16[2048,1024]{1,0:T(8,128)(2,1)} %subtract_convert_fusion, bf16[512,2048]{1,0:T(8,128)(2,1)S(1)} %bitcast.37), kind=kOutput, calls=%fused_computation.15 | convolution fusion | flops 4303355904 | bytes 11534336 | tf_op jit(solution)/shard_map/dot_general | solution.py:74
  262.0 106.3 %all-reduce.7.cloned.1.call-done = f32[512,2048]{1,0:T(8,128)} async-done(((f32[512,2048]{1,0:T(8,128)}), f32[512,2048]{1,0:T(8,128)}) %all-reduce.7.cloned.1.call-update) | async-done | bytes 4194320 | tf_op jit(solution)/shard_map/psum | solution.py:77
  368.4 4.5 subtract_convert_fusion.1
  372.9 9.7 %fusion.5 = f32[512,1024]{0,1:T(8,128)} fusion(bf16[512,2048]{1,0:T(8,128)(2,1)} %subtract_convert_fusion.1, bf16[2048,1024]{1,0:T(8,128)(2,1)} %subtract_convert_fusion, bf16[512,1024]{0,1:T(8,128)(2,1)S(1)} %subtract_convert_fusion.3), kind=kOutput, calls=%fused_computation.14 | convolution fusion | flops 4303355904 | bytes 9437184 | tf_op jit(solution)/shard_map/dot_general | solution.py:67
  382.9 142.6 %all-reduce.9.cloned.1.call-done = f32[512,1024]{0,1:T(8,128)} async-done(((f32[512,1024]{0,1:T(8,128)}), f32[512,1024]{0,1:T(8,128)}) %all-reduce.9.cloned.1.call-update) | async-done | bytes 2097168 | tf_op jit(solution)/shard_map/psum | solution.py:66
  525.5 3.0 subtract_convert_fusion.2
  528.5 9.6 %fusion.4 = f32[512,2048]{1,0:T(8,128)} fusion(bf16[512,1024]{0,1:T(8,128)(2,1)} %subtract_convert_fusion.2, bf16[2048,1024]{1,0:T(8,128)(2,1)} %subtract_convert_fusion, bf16[512,2048]{1,0:T(8,128)(2,1)S(1)} %copy-done), kind=kOutput, calls=%fused_computation.13 | convolution fusion | flops 4303355904 | bytes 11534336 | tf_op jit(solution)/shard_map/dot_general | solution.py:74
  538.4 1.1 constant_dynamic-slice_fusion
  539.5 0.8 copy.15
  540.2 104.9 %all-reduce.11.cloned.1.call-done = f32[512,2048]{1,0:T(8,128)} async-done(((f32[512,2048]{1,0:T(8,128)}), f32[512,2048]{1,0:T(8,128)}) %all-reduce.11.cloned.1.call-update) | async-done | bytes 4194320 | tf_op jit(solution)/shard_map/psum | solution.py:77
  645.2 1.9 subtract_convert_fusion.4
  (34 shorter events, 2.3 us)
Async XLA Ops:
  7.2 18.6 %copy-start.2 = (s32[8]{0:T(128)S(1)}, s32[8]{0:T(128)}, u32[]{:S(2)}) copy-start(s32[8]{0:T(128)} %param.9) | copy-start | bytes 100
  7.2 86.8 %all-gather.2.cloned.1.call-start = ((), (), s32[]{:S(2)}) async-start(), calls=%async_computation.1 | async-start | bytes 1114112 | tf_op jit(solution)/shard_map/all_gather | solution.py:59
  10.4 83.6 %all-to-all-start = ((bf16[8,64,2048]{2,1,0:T(8,128)(2,1)}), bf16[8,64,2048]{2,1,0:T(8,128)(2,1)S(1)}, u32[]{:S(2)}, u32[]{:S(2)}) async-start(bf16[8,64,2048]{2,1,0:T(8,128)(2,1)} %stack.2), calls=%async_computation | async-start | bytes 4194304 | tf_op jit(solution)/shard_map/all_to_all | solution.py:57
  17.3 232.5 %all-reduce.5.cloned.1.call-start = ((), (), s32[]{:S(2)}) async-start(), calls=%async_computation.2 | async-start | bytes 4194304 | tf_op jit(solution)/shard_map/psum | solution.py:66
  18.5 31.7 %collective-permute-start = (bf16[129,1024]{1,0:T(8,128)(2,1)S(1)}, bf16[129,1024]{1,0:T(8,128)(2,1)S(1)}, u32[]{:S(2)}, u32[]{:S(2)}) collective-permute-start(bf16[129,1024]{1,0:T(8,128)(2,1)S(1)} %get-tuple-element.7), channel_id=1, source_target_pairs={{0,8},{8,16},{16,24},{24,32},{32,40},{40,48},{48,56},{56,64},{64,7... | collective-permute-start | bytes 792584 | tf_op jit(solution)/shard_map/ppermute | solution.py:19
  23.9 26.3 %collective-permute-start.1 = (bf16[129,1024]{1,0:T(8,128)(2,1)S(1)}, bf16[129,1024]{1,0:T(8,128)(2,1)S(1)}, u32[]{:S(2)}, u32[]{:S(2)}) collective-permute-start(bf16[129,1024]{1,0:T(8,128)(2,1)S(1)} %get-tuple-element.6), channel_id=1, source_target_pairs={{8,0},{16,8},{24,16},{32,24},{40,32},{48,40},{56,48},{64,56},{72,6... | collective-permute-start | bytes 792584 | tf_op jit(solution)/shard_map/ppermute | solution.py:20
  94.0 9.1 %copy-start.3 = (f32[512]{0:T(512)S(1)}, f32[512]{0:T(512)}, u32[]{:S(2)}) copy-start(f32[512]{0:T(512)} %param.15) | copy-start | bytes 6148
  94.0 9.1 %copy-start.5 = (f32[512]{0:T(512)S(1)}, f32[512]{0:T(512)}, u32[]{:S(2)}) copy-start(f32[512]{0:T(512)} %param.13) | copy-start | bytes 6148
  94.1 9.1 %copy-start.1 = (bf16[512,1024]{1,0:T(8,128)(2,1)S(1)}, bf16[512,1024]{1,0:T(8,128)(2,1)}, u32[]{:S(2)}) copy-start(bf16[512,1024]{1,0:T(8,128)(2,1)} %all-gather.2.cloned.1.call-done) | copy-start | bytes 3145732
  102.8 265.5 %all-reduce.7.cloned.1.call-start = ((), (), s32[]{:S(2)}) async-start(), calls=%async_computation.3 | async-start | bytes 8388608 | tf_op jit(solution)/shard_map/psum | solution.py:77
  261.3 0.7 copy-start.4
  261.3 0.7 copy-start.6
  261.4 264.1 %all-reduce.9.cloned.1.call-start = ((), (), s32[]{:S(2)}) async-start(), calls=%async_computation.4 | async-start | bytes 4194304 | tf_op jit(solution)/shard_map/psum | solution.py:66
  382.6 145.9 %copy-start = (bf16[512,2048]{1,0:T(8,128)(2,1)S(1)}, bf16[512,2048]{1,0:T(8,128)(2,1)}, u32[]{:S(2)}) copy-start(bf16[512,2048]{1,0:T(8,128)(2,1)} %subtract_convert_fusion.1) | copy-start | bytes 6291460
  382.6 262.6 %all-reduce.11.cloned.1.call-start = ((), (), s32[]{:S(2)}) async-start(), calls=%async_computation.5 | async-start | bytes 8388608 | tf_op jit(solution)/shard_map/psum | solution.py:77
Sparse Core Ops, SparseCore 0:
  10.4 52.1 all-gather.1
  103.0 146.7 all-reduce.4
  261.5 106.8 all-reduce.6
  382.7 142.7 all-reduce.8
  538.3 106.8 all-reduce.10
